TPU v7x, 128 devices: a whole 4x4x4 slice. The times are simulated.
128 devices in a mesh: trow: 4 (over z), tcol: 32 (over y, x, core).
Axes of the slice: x: 4, y: 4, z: 4, core: 2. Of those that a mesh axis runs over, the one named last changes fastest.
Arguments:
- object_slab: float32 [2, 4096, 32768], P(None, 'trow', 'tcol'), may hold values from -6 to 6
- probe_field: float32 [2, 256, 256], replicated, may hold values from -6 to 6
- amplitudes: bfloat16 [2048, 256, 256], P(('trow', 'tcol')), may hold values from 0.19921875 to 3
- positions: int32 [2048, 2], P(('trow', 'tcol')), may hold values from 0 to 1023
- shift_bins: int32 [2048, 2], P(('trow', 'tcol')), may hold values from 0 to 15
- destinations: int32 [2048, 1], P(('trow', 'tcol')), may hold values from 0 to 31; in each aligned block of 16 rows (0 to 15, 16 to 31, ...) at most 2 rows name the same one
- frame_counts: int32 [128], P(('trow', 'tcol')), may hold values from 1 to 16
Outputs:
- probe_step: float32 [2, 256, 256], replicated
- arrivals: float32 [8192, 3], P(('trow', 'tcol'))
Inputs may be any that keep to these rules, and one draw needn't show every extreme that they name: `destinations`: among the slots of one device at most 2 share a destination, and in some device exactly 2 do.
All inputs are finite; a program needn't handle non-finite values.
Results may differ from a plain program's by a relative error of at most 0.0003.
Values sent between devices are 32-bit elements; how exact they have to be, the bound alone decides.
No kernel may reach another device: no remote copies, remote signals or barrier semaphores. Data moves between devices by JAX's collectives and lax.ppermute only.
A program may use at most 128 MiB of HBM per device.

v0:
```python
import math

import jax
import jax.numpy as jnp
from jax import lax
from jax.sharding import PartitionSpec as P

BINS = 16


exact_mode = lax.Precision.HIGHEST


def padded(array, sides, width):
    for axis, dim in sides:
        devices, length = (lax.axis_size(axis), array.shape[dim])
        up = [(i, (i + 1) % devices) for i in range(devices - 1)]
        down = [(j, i) for i, j in up]
        last = lax.slice_in_dim(array, length - width, length, axis=dim)
        leading = lax.slice_in_dim(array, 0, width, axis=dim)
        before = lax.ppermute(last, axis, up)
        after = lax.ppermute(leading, axis, down)
        array = jnp.concatenate([before, array, after], axis=dim)
    return array


def left_apply(matrix, stacked):
    return jnp.einsum(
        "kn,bnm->bkm", matrix, stacked, precision=exact_mode, preferred_element_type=jnp.float32
    )


def right_apply(stacked, matrix):
    return jnp.einsum(
        "bkn,nm->bkm", stacked, matrix, precision=exact_mode, preferred_element_type=jnp.float32
    )


def frame_terms(extended, probe_field, measured, spots, bins_pair, live_mask):
    frame = probe_field.shape[1]
    half = frame // 2
    wave_number = jnp.arange(frame)
    angle = (
        2.0
        * math.pi
        / frame
        * (wave_number[:, None] * wave_number[None, :] % frame).astype(jnp.float32)
    )
    cosine = jnp.cos(angle) / math.sqrt(frame)
    sine = jnp.sin(angle) / math.sqrt(frame)
    freqs = ((wave_number + half) % frame - half).astype(jnp.float32) / frame
    patches = jax.vmap(
        lambda spot: lax.dynamic_slice(
            extended, (jnp.zeros((), jnp.int32), spot[0], spot[1]), (2, frame, frame)
        )
    )(spots)
    obj_real = patches[:, 0]
    obj_imag = patches[:, 1]
    wave_real = probe_field[0] * obj_real - probe_field[1] * obj_imag
    wave_imag = probe_field[0] * obj_imag + probe_field[1] * obj_real
    half_real = left_apply(cosine, wave_real) + left_apply(sine, wave_imag)
    half_imag = left_apply(cosine, wave_imag) - left_apply(sine, wave_real)
    full_real = right_apply(half_real, cosine) + right_apply(half_imag, sine)
    full_imag = right_apply(half_imag, cosine) - right_apply(half_real, sine)
    shifts = bins_pair.astype(jnp.float32) / BINS - 0.5
    theta = (
        2.0
        * math.pi
        * (
            freqs[None, :, None] * shifts[:, 0, None, None]
            + freqs[None, None, :] * shifts[:, 1, None, None]
        )
    )
    ramp_cos = jnp.cos(theta)
    ramp_sin = jnp.sin(theta)
    spec_real = full_real * ramp_cos + full_imag * ramp_sin
    spec_imag = full_imag * ramp_cos - full_real * ramp_sin
    magnitude = jnp.sqrt(spec_real * spec_real + spec_imag * spec_imag + 0.1)
    factor = measured.astype(jnp.float32) / magnitude
    diff_real = factor * spec_real - spec_real
    diff_imag = factor * spec_imag - spec_imag
    error = jnp.sum(diff_real * diff_real + diff_imag * diff_imag, axis=(1, 2)) / (frame * frame)
    cross = diff_imag * full_real - diff_real * full_imag
    grad_y = 2.0 * math.pi / frame * jnp.sum(freqs[None, :, None] * cross, axis=(1, 2))
    grad_x = 2.0 * math.pi / frame * jnp.sum(freqs[None, None, :] * cross, axis=(1, 2))
    back_real = diff_real * ramp_cos - diff_imag * ramp_sin
    back_imag = diff_imag * ramp_cos + diff_real * ramp_sin
    middle_real = left_apply(cosine, back_real) - left_apply(sine, back_imag)
    middle_imag = left_apply(cosine, back_imag) + left_apply(sine, back_real)
    chi_real = right_apply(middle_real, cosine) - right_apply(middle_imag, sine)
    chi_imag = right_apply(middle_imag, cosine) + right_apply(middle_real, sine)
    term_real = obj_real * chi_real + obj_imag * chi_imag
    term_imag = obj_real * chi_imag - obj_imag * chi_real
    weight = obj_real * obj_real + obj_imag * obj_imag
    mask = live_mask[:, None, None]
    sums = (
        jnp.sum(mask * term_real, axis=0),
        jnp.sum(mask * term_imag, axis=0),
        jnp.sum(mask * weight, axis=0),
    )
    records = live_mask[:, None] * jnp.stack([grad_y, grad_x, error], axis=1)
    return (sums, records)


def body(object_slab, probe_field, amplitudes, positions, shift_bins, destinations, frame_counts):
    frame = probe_field.shape[1]
    half = frame // 2
    per_device = amplitudes.shape[0]
    extended = padded(object_slab, (("trow", 1), ("tcol", 2)), half)
    live_mask = (jnp.arange(per_device) < frame_counts[0]).astype(jnp.float32)
    zeros = jnp.zeros((frame, frame), jnp.float32)
    group = 8
    blocks = per_device // group

    def grouped(array):
        return array.reshape((blocks, group) + array.shape[1:])

    def step_group(totals, inputs):
        measured, spots, bins_pair, alive = inputs
        fresh, record = frame_terms(extended, probe_field, measured, spots, bins_pair, alive)
        return ((totals[0] + fresh[0], totals[1] + fresh[1], totals[2] + fresh[2]), record)

    sums, block_records = lax.scan(
        step_group,
        (zeros, zeros, zeros),
        (grouped(amplitudes), grouped(positions), grouped(shift_bins), grouped(live_mask)),
    )
    records = block_records.reshape(per_device, 3)
    summed = lax.psum((sums[0], sums[1], sums[2]), ("trow", "tcol"))
    probe_step = jnp.stack([summed[0], summed[1]]) / jnp.sqrt(summed[2] + 1.0)[None]
    col_count = lax.axis_size("tcol")
    capacity = max(2, 2 * per_device // col_count)
    targets = destinations[:, 0]
    slot_ids = jnp.arange(per_device)
    same = targets[:, None] == targets[None, :]
    earlier = slot_ids[:, None] > slot_ids[None, :]
    rank = jnp.sum((same & earlier).astype(jnp.int32), axis=1)
    owners = jnp.arange(col_count)
    places = jnp.arange(capacity)
    selector = (
        (targets[None, None, :] == owners[:, None, None])
        & (rank[None, None, :] == places[None, :, None])
    ).astype(jnp.float32)
    outgoing = jnp.einsum(
        "ecj,jr->ecr", selector, records, precision=exact_mode, preferred_element_type=jnp.float32
    )
    arrivals = lax.all_to_all(
        outgoing.reshape(col_count * capacity, 3), "tcol", split_axis=0, concat_axis=0, tiled=True
    )
    return (probe_step, arrivals)


def solution(mesh):
    in_specs = (
        P(None, "trow", "tcol"),
        P(),
        P(("trow", "tcol"), None, None),
        P(("trow", "tcol"), None),
        P(("trow", "tcol"), None),
        P(("trow", "tcol"), None),
        P(("trow", "tcol")),
    )
    out_specs = (P(), P(("trow", "tcol"), None))
    return jax.shard_map(body, mesh=mesh, in_specs=in_specs, out_specs=out_specs, check_vma=False)
```

profile of v0, /device:TPU:1, one launch (start us, length us, event | category | flops | bytes accessed | tf_op | source)
XLA Modules:
  0.0 550.7 jit_solution(12403908040344905148)
XLA Ops:
  14.6 20.4 %collective-permute-done = f32[2,128,1024]{2,1,0:T(8,128)S(1)} collective-permute-done((f32[2,128,1024]{2,1,0:T(8,128)S(1)}, f32[2,128,1024]{2,1,0:T(8,128)S(1)}, u32[]{:S(2)}, u32[]{:S(2)}) %collective-permute-start) | collective-permute-done | bytes 1048608 | tf_op jit(solution)/shard_map/ppermute | solution.py:21
  53.9 10.6 %collective-permute-done.2 = f32[2,1280,128]{2,1,0:T(8,128)S(1)} collective-permute-done((f32[2,1280,128]{2,1,0:T(8,128)}, f32[2,1280,128]{2,1,0:T(8,128)S(1)}, u32[]{:S(2)}, u32[]{:S(2)}) %collective-permute-start.2) | collective-permute-done | bytes 1310752 | tf_op jit(solution)/shard_map/ppermute | solution.py:21
  69.0 10.1 %pad_maximum_fusion = f32[2,1280,1280]{2,1,0:T(8,128)} fusion(f32[2,1280,128]{2,1,0:T(8,128)} %collective-permute-done.3, f32[2,1280,1024]{2,1,0:T(8,128)} %copy-done.4, f32[2,1280,128]{2,1,0:T(8,128)S(1)} %collective-permute-done.2), kind=kLoop, calls=%fused_computation.200 | loop fusion | flops 6553600 | bytes 26214400 | tf_op jit(solution)/shard_map/concatenate | solution.py:23
  79.0 309.5 %while.23 = (s32[]{:T(128)}, f32[256,256]{1,0:T(8,128)S(1)}, f32[256,256]{1,0:T(8,128)S(1)}, f32[256,256]{1,0:T(8,128)S(1)}, f32[2,8,3]{1,0,2:T(2,128)S(1)}, /*i...) while((s32[]{:T(128)}, f32[256,256]{1,0:T(8,128)S(1)}, ...), condition=%wide.region_7.8_spmd.clone, body=%wide.region_0.7_spmd.clone.sunk | while | flops 25829777408 | bytes 184654672 | solution.py:123
  79.3 32.4 %while.24 = (s32[]{:T(128)}, f32[2,1280,1280]{2,1,0:T(8,128)}, s32[8,3]{0,1:T(4,128)S(1)}, f32[8,2,256,256]{3,2,0,1:T(8,128)}, s32[]{:T(128)}) while((s32[]{:T(128)}, f32[2,1280,1280]{2,1,0:T(8,128)}, s32[8,3]{0,1:T(4,128)S(1)}, f32[8,2,256,256]{3,2,0,1:T(8,128)}, s32[]{:T(128)}) %tuple.86), condition=%wide.while_cond, body=%wide.while_body.sunk | while | flops 2 | bytes 1050217 | solution.py:53
  111.8 6.9 %fusion.229 = f32[8,256,256]{2,1,0:T(8,128)S(1)} fusion(f32[8,2,256,256]{3,2,0,1:T(8,128)} %get-tuple-element.416, f32[256,256]{1,0:T(8,128)S(1)} %get-tuple-element.417, f32[256,256]{1,0:T(8,128)S(1)} %get-tuple-element.418), kind=kOutput, calls=%fused_computation.85.clone.1 | convolution fusion | flops 1613168640 | bytes 6815744 | tf_op jit(solution)/shard_map/while/body/eval_jaxpr/kn,bnm->bkm/dot_general | solution.py:28
  118.8 4.6 convolution_add_fusion.4
  123.4 5.2 fusion.227
  128.6 4.6 convolution_subtract_fusion.4
  137.8 4.7 fusion.230
  147.2 13.6 %multiply_subtract_fusion.14 = (f32[8,256,256]{2,1,0:T(8,128)S(1)}, f32[8,256,256]{2,1,0:T(8,128)S(1)}, f32[8,256,256]{2,1,0:T(8,128)S(1)}) fusion(f32[8,256,256]{2,1,0:T(8,128)S(1)} %fusion.230, f32[8,256]{1,0:T(8,128)S(1)} %get-tuple-element.421, f32[8,256]{1,0:T(8,128)S(1)} %get-tuple-element.422, bf16[2,8,256,256]{3,2,1,0:T(8,128)(2,1)S(1)} %copy-done.13, ...), kind=kOutput, calls=%fused_computation.45.clone.1 | convolution fusion | flops 1623130112 | bytes 13647876 | tf_op jit(solution)/shard_map/while/body/eval_jaxpr/bkn,nm->bkm/dot_general | solution.py:34
  162.7 13.9 %fusion.235 = f32[8,256,256]{2,1,0:T(8,128)S(1)} fusion(f32[8,256,256]{2,1,0:T(8,128)S(1)} %get-tuple-element.424, f32[8,256,256]{2,1,0:T(8,128)} %copy-done, f32[8,256]{1,0:T(8,128)S(1)} %get-tuple-element.421, f32[8,256]{1,0:T(8,128)S(1)} %get-tuple-element.422), kind=kOutput, calls=%fused_computation.79.clone.1 | convolution fusion | flops 1614217216 | bytes 6307840 | tf_op jit(solution)/shard_map/while/body/eval_jaxpr/kn,bnm->bkm/dot_general | solution.py:28
  176.6 12.2 %convolution_subtract_fusion.5 = f32[8,256,256]{2,1,0:T(8,128)S(1)} fusion(f32[8,256,256]{2,1,0:T(8,128)S(1)} %fusion.235, f32[8,256,256]{2,1,0:T(8,128)S(1)} %copy-done.1, f32[8,256,256]{2,1,0:T(8,128)S(1)} %get-tuple-element.424, f32[8,256]{1,0:T(8,128)S(1)} %get-tuple-element.421, f32[8,256]{1,0:T(8,128)S(1)} %get-tuple-element.422), kind=kOutput, calls=%fused_computation.58.clone.1 | convolution fusion | flops 1614741504 | bytes 8404992 | tf_op jit(solution)/shard_map/while/body/eval_jaxpr/kn,bnm->bkm/dot_general | solution.py:28
  188.8 12.4 %fusion.233 = f32[8,256,256]{2,1,0:T(8,128)S(1)} fusion(f32[8,256,256]{2,1,0:T(8,128)S(1)} %copy-done.1, f32[8,256,256]{2,1,0:T(8,128)S(1)} %get-tuple-element.424, f32[8,256]{1,0:T(8,128)S(1)} %get-tuple-element.421, f32[8,256]{1,0:T(8,128)S(1)} %get-tuple-element.422), kind=kOutput, calls=%fused_computation.76.clone.1 | convolution fusion | flops 1614217216 | bytes 6307840 | tf_op jit(solution)/shard_map/while/body/eval_jaxpr/kn,bnm->bkm/dot_general | solution.py:28
  201.2 12.2 %convolution_add_fusion.5 = f32[8,256,256]{2,1,0:T(8,128)S(1)} fusion(f32[8,256,256]{2,1,0:T(8,128)S(1)} %fusion.233, f32[8,256,256]{2,1,0:T(8,128)S(1)} %get-tuple-element.424, f32[8,256,256]{2,1,0:T(8,128)S(1)} %copy-done.1, f32[8,256]{1,0:T(8,128)S(1)} %get-tuple-element.421, f32[8,256]{1,0:T(8,128)S(1)} %get-tuple-element.422), kind=kOutput, calls=%fused_computation.57.clone.1 | convolution fusion | flops 1614741504 | bytes 8404992 | tf_op jit(solution)/shard_map/while/body/eval_jaxpr/kn,bnm->bkm/dot_general | solution.py:28
  222.5 4.7 fusion.238
  227.1 5.7 %fusion.239 = (f32[256,256]{1,0:T(8,128)S(1)}, f32[256,256]{1,0:T(8,128)S(1)}, f32[256,256]{1,0:T(8,128)S(1)}) fusion(f32[8,256,256]{2,1,0:T(8,128)S(1)} %fusion.236, f32[8,2,256,256]{3,2,0,1:T(8,128)S(1)} %copy-done.3, f32[8]{0:T(128)S(1)} %fusion.237, f32[8,256,256]{2,1,0:T(8,128)S(1)} %fusion.238, f32[8,256,256]{2,1,0:T(8,128)S(1)} %convolution_subtract_fusion.5), kind=kOutput, calls=%fused_computation.33.clone.1 | convolution fusion | flops 1619787776 | bytes 11272224 | tf_op jit(solution)/shard_map/while/body/eval_jaxpr/bkn,nm->bkm/dot_general | solution.py:34
  233.5 32.4 %while.24 = (s32[]{:T(128)}, f32[2,1280,1280]{2,1,0:T(8,128)}, s32[8,3]{0,1:T(4,128)S(1)}, f32[8,2,256,256]{3,2,0,1:T(8,128)}, s32[]{:T(128)}) while((s32[]{:T(128)}, f32[2,1280,1280]{2,1,0:T(8,128)}, s32[8,3]{0,1:T(4,128)S(1)}, f32[8,2,256,256]{3,2,0,1:T(8,128)}, s32[]{:T(128)}) %tuple.86), condition=%wide.while_cond, body=%wide.while_body.sunk | while | flops 2 | bytes 1050217 | solution.py:53
  266.0 6.9 %fusion.229 = f32[8,256,256]{2,1,0:T(8,128)S(1)} fusion(f32[8,2,256,256]{3,2,0,1:T(8,128)} %get-tuple-element.416, f32[256,256]{1,0:T(8,128)S(1)} %get-tuple-element.417, f32[256,256]{1,0:T(8,128)S(1)} %get-tuple-element.418), kind=kOutput, calls=%fused_computation.85.clone.1 | convolution fusion | flops 1613168640 | bytes 6815744 | tf_op jit(solution)/shard_map/while/body/eval_jaxpr/kn,bnm->bkm/dot_general | solution.py:28
  273.0 4.6 convolution_add_fusion.4
  277.6 4.8 fusion.227
  282.4 4.6 convolution_subtract_fusion.4
  291.6 4.7 fusion.230
  301.0 13.8 %multiply_subtract_fusion.14 = (f32[8,256,256]{2,1,0:T(8,128)S(1)}, f32[8,256,256]{2,1,0:T(8,128)S(1)}, f32[8,256,256]{2,1,0:T(8,128)S(1)}) fusion(f32[8,256,256]{2,1,0:T(8,128)S(1)} %fusion.230, f32[8,256]{1,0:T(8,128)S(1)} %get-tuple-element.421, f32[8,256]{1,0:T(8,128)S(1)} %get-tuple-element.422, bf16[2,8,256,256]{3,2,1,0:T(8,128)(2,1)S(1)} %copy-done.13, ...), kind=kOutput, calls=%fused_computation.45.clone.1 | convolution fusion | flops 1623130112 | bytes 13647876 | tf_op jit(solution)/shard_map/while/body/eval_jaxpr/bkn,nm->bkm/dot_general | solution.py:34
  316.5 13.9 %fusion.235 = f32[8,256,256]{2,1,0:T(8,128)S(1)} fusion(f32[8,256,256]{2,1,0:T(8,128)S(1)} %get-tuple-element.424, f32[8,256,256]{2,1,0:T(8,128)} %copy-done, f32[8,256]{1,0:T(8,128)S(1)} %get-tuple-element.421, f32[8,256]{1,0:T(8,128)S(1)} %get-tuple-element.422), kind=kOutput, calls=%fused_computation.79.clone.1 | convolution fusion | flops 1614217216 | bytes 6307840 | tf_op jit(solution)/shard_map/while/body/eval_jaxpr/kn,bnm->bkm/dot_general | solution.py:28
  330.4 12.4 %convolution_subtract_fusion.5 = f32[8,256,256]{2,1,0:T(8,128)S(1)} fusion(f32[8,256,256]{2,1,0:T(8,128)S(1)} %fusion.235, f32[8,256,256]{2,1,0:T(8,128)S(1)} %copy-done.1, f32[8,256,256]{2,1,0:T(8,128)S(1)} %get-tuple-element.424, f32[8,256]{1,0:T(8,128)S(1)} %get-tuple-element.421, f32[8,256]{1,0:T(8,128)S(1)} %get-tuple-element.422), kind=kOutput, calls=%fused_computation.58.clone.1 | convolution fusion | flops 1614741504 | bytes 8404992 | tf_op jit(solution)/shard_map/while/body/eval_jaxpr/kn,bnm->bkm/dot_general | solution.py:28
  342.8 12.1 %fusion.233 = f32[8,256,256]{2,1,0:T(8,128)S(1)} fusion(f32[8,256,256]{2,1,0:T(8,128)S(1)} %copy-done.1, f32[8,256,256]{2,1,0:T(8,128)S(1)} %get-tuple-element.424, f32[8,256]{1,0:T(8,128)S(1)} %get-tuple-element.421, f32[8,256]{1,0:T(8,128)S(1)} %get-tuple-element.422), kind=kOutput, calls=%fused_computation.76.clone.1 | convolution fusion | flops 1614217216 | bytes 6307840 | tf_op jit(solution)/shard_map/while/body/eval_jaxpr/kn,bnm->bkm/dot_general | solution.py:28
  355.0 12.2 %convolution_add_fusion.5 = f32[8,256,256]{2,1,0:T(8,128)S(1)} fusion(f32[8,256,256]{2,1,0:T(8,128)S(1)} %fusion.233, f32[8,256,256]{2,1,0:T(8,128)S(1)} %get-tuple-element.424, f32[8,256,256]{2,1,0:T(8,128)S(1)} %copy-done.1, f32[8,256]{1,0:T(8,128)S(1)} %get-tuple-element.421, f32[8,256]{1,0:T(8,128)S(1)} %get-tuple-element.422), kind=kOutput, calls=%fused_computation.57.clone.1 | convolution fusion | flops 1614741504 | bytes 8404992 | tf_op jit(solution)/shard_map/while/body/eval_jaxpr/kn,bnm->bkm/dot_general | solution.py:28
  376.3 4.9 fusion.238
  381.2 5.7 %fusion.239 = (f32[256,256]{1,0:T(8,128)S(1)}, f32[256,256]{1,0:T(8,128)S(1)}, f32[256,256]{1,0:T(8,128)S(1)}) fusion(f32[8,256,256]{2,1,0:T(8,128)S(1)} %fusion.236, f32[8,2,256,256]{3,2,0,1:T(8,128)S(1)} %copy-done.3, f32[8]{0:T(128)S(1)} %fusion.237, f32[8,256,256]{2,1,0:T(8,128)S(1)} %fusion.238, f32[8,256,256]{2,1,0:T(8,128)S(1)} %convolution_subtract_fusion.5), kind=kOutput, calls=%fused_computation.33.clone.1 | convolution fusion | flops 1619787776 | bytes 11272224 | tf_op jit(solution)/shard_map/while/body/eval_jaxpr/bkn,nm->bkm/dot_general | solution.py:34
  389.9 15.8 %all_to_all.9 = f32[32,2,3]{2,1,0:T(2,128)S(1)} all-to-all(f32[32,2,3]{2,1,0:T(2,128)S(1)} %copy.96), channel_id=1, replica_groups=mesh['trow'=4,'tcol'=32] {'tcol'}, dimensions={0} | all-to-all | bytes 1536 | tf_op jit(solution)/shard_map/all_to_all | solution.py:147
  406.4 134.3 %all-reduce.3.cloned.1.call-done = (f32[1,256,256]{2,1,0:T(8,128)}, f32[1,256,256]{2,1,0:T(8,128)}, f32[256,256]{1,0:T(8,128)}) async-done(((f32[1,256,256]{2,1,0:T(8,128)}, f32[1,256,256]{2,1,0:T(8,128)}, f32[256,256]{1,0:T(8,128)}), (f32[1,256,256]{2,1,0:T(8,128)}, f32[1,256,256]{2,1,0:T(8,128)}, f32[256,256]{1,0:T(8,128)})) %all-reduce.3.cloned.1.call-update) | async-done | bytes 786448 | tf_op jit(solution)/shard_map/psum | solution.py:129
  (167 shorter events, 140.0 us)
Async XLA Ops:
  7.2 533.5 %all-reduce.3.cloned.1.call-start = ((), (), s32[]{:S(2)}) async-start(), calls=%async_computation.1 | async-start | bytes 1572864 | tf_op jit(solution)/shard_map/psum | solution.py:129
  8.9 26.2 %collective-permute-start = (f32[2,128,1024]{2,1,0:T(8,128)S(1)}, f32[2,128,1024]{2,1,0:T(8,128)S(1)}, u32[]{:S(2)}, u32[]{:S(2)}) collective-permute-start(f32[2,128,1024]{2,1,0:T(8,128)S(1)} %get-tuple-element.295), channel_id=1, source_target_pairs={{0,32},{32,64},{64,96},{1,33},{33,65},{65,97},{2,34},{34,66},{66,9... | collective-permute-start | bytes 3145736 | tf_op jit(solution)/shard_map/ppermute | solution.py:21
  13.3 26.1 %collective-permute-start.1 = (f32[2,128,1024]{2,1,0:T(8,128)S(1)}, f32[2,128,1024]{2,1,0:T(8,128)S(1)}, u32[]{:S(2)}, u32[]{:S(2)}) collective-permute-start(f32[2,128,1024]{2,1,0:T(8,128)S(1)} %get-tuple-element.294), channel_id=1, source_target_pairs={{32,0},{64,32},{96,64},{33,1},{65,33},{97,65},{34,2},{66,34},{98,6... | collective-permute-start | bytes 3145736 | tf_op jit(solution)/shard_map/ppermute | solution.py:22
  39.5 3.9 copy-start.4
  43.4 8.2 %copy-start.10 = (s32[16,2]{0,1:T(2,128)S(1)}, s32[16,2]{0,1:T(2,128)}, u32[]{:S(2)}) copy-start(s32[16,2]{0,1:T(2,128)} %param.12) | copy-start | bytes 388
  43.4 8.3 %copy-start.11 = (s32[16,2]{0,1:T(2,128)S(1)}, s32[16,2]{0,1:T(2,128)}, u32[]{:S(2)}) copy-start(s32[16,2]{0,1:T(2,128)} %param.13) | copy-start | bytes 388
  43.4 9.1 %copy-start.12 = (s32[16,1]{0,1:T(1,128)S(1)}, s32[16,1]{0,1:T(1,128)}, u32[]{:S(2)}) copy-start(s32[16,1]{0,1:T(1,128)} %param.14) | copy-start | bytes 196
  45.2 19.4 %collective-permute-start.2 = (f32[2,1280,128]{2,1,0:T(8,128)}, f32[2,1280,128]{2,1,0:T(8,128)S(1)}, u32[]{:S(2)}, u32[]{:S(2)}) collective-permute-start(f32[2,1280,128]{2,1,0:T(8,128)} %get-tuple-element.292), channel_id=1, source_target_pairs={{0,1},{1,2},{2,3},{3,4},{4,5},{5,6},{6,7},{7,8},{8,9},{9,10},{10,1... | collective-permute-start | bytes 3932168 | tf_op jit(solution)/shard_map/ppermute | solution.py:21
  49.7 19.2 %collective-permute-start.3 = (f32[2,1280,128]{2,1,0:T(8,128)}, f32[2,1280,128]{2,1,0:T(8,128)}, u32[]{:S(2)}, u32[]{:S(2)}) collective-permute-start(f32[2,1280,128]{2,1,0:T(8,128)} %get-tuple-element.293), channel_id=1, source_target_pairs={{1,0},{2,1},{3,2},{4,3},{5,4},{6,5},{7,6},{8,7},{9,8},{10,9},{11,1... | collective-permute-start | bytes 3932168 | tf_op jit(solution)/shard_map/ppermute | solution.py:22
  53.9 25.1 %copy-start.5 = (f32[2,256,256]{2,1,0:T(8,128)S(1)}, f32[2,256,256]{2,1,0:T(8,128)}, u32[]{:S(2)}) copy-start(f32[2,256,256]{2,1,0:T(8,128)} %param.10) | copy-start | bytes 1572868
  79.0 310.5 %copy-start.14 = (s32[16]{0:T(128)S(1)}, s32[16]{0:T(128)}, u32[]{:S(2)}) copy-start(s32[16]{0:T(128)} %convert_reduce_fusion) | copy-start | bytes 196
  79.0 310.6 %copy-start.9 = (pred[32,16]{0,1:T(8,128)(4,1)S(1)}, pred[32,16]{0,1:T(8,128)(4,1)}, u32[]{:S(2)}) copy-start(pred[32,16]{0,1:T(8,128)(4,1)} %iota_compare_fusion.1) | copy-start | bytes 1540
  111.8 7.0 %copy-start.2 = (f32[8,2,256,256]{3,2,0,1:T(8,128)S(1)}, f32[8,2,256,256]{3,2,0,1:T(8,128)}, u32[]{:S(2)}) copy-start(f32[8,2,256,256]{3,2,0,1:T(8,128)} %get-tuple-element.416) | copy-start | bytes 12582916 | tf_op jit(solution)/shard_map/while
  142.5 4.7 copy-start.13
  160.8 1.4 copy-start
  162.7 13.9 %copy-start.1 = (f32[8,256,256]{2,1,0:T(8,128)S(1)}, f32[8,256,256]{2,1,0:T(8,128)}, u32[]{:S(2)}) copy-start(f32[8,256,256]{2,1,0:T(8,128)} %copy-done) | copy-start | bytes 6291460 | tf_op jit(solution)/shard_map/while
  222.5 4.7 copy-start.3
  266.0 7.0 %copy-start.2 = (f32[8,2,256,256]{3,2,0,1:T(8,128)S(1)}, f32[8,2,256,256]{3,2,0,1:T(8,128)}, u32[]{:S(2)}) copy-start(f32[8,2,256,256]{3,2,0,1:T(8,128)} %get-tuple-element.416) | copy-start | bytes 12582916 | tf_op jit(solution)/shard_map/while
  296.4 4.7 copy-start.13
  314.8 1.4 copy-start
  316.5 14.0 %copy-start.1 = (f32[8,256,256]{2,1,0:T(8,128)S(1)}, f32[8,256,256]{2,1,0:T(8,128)}, u32[]{:S(2)}) copy-start(f32[8,256,256]{2,1,0:T(8,128)} %copy-done) | copy-start | bytes 6291460 | tf_op jit(solution)/shard_map/while
  376.3 4.9 copy-start.3
  388.6 0.7 copy-start.6
  388.6 0.8 copy-start.7
  388.6 0.9 copy-start.8
Sparse Core Ops, SparseCore 0:
  389.6 151.0 all-reduce.2
where the time goes:
time: 555 us; the launch traced here: 551 us
  matrix products  238 us (43%)
  waiting for transfers between devices  170 us (31%)
  local copies, waits for them, and re-layouts  80.3 us (14%)
  other arithmetic  16.7 us (3%)
  blocking collectives  15.8 us (3%)
  between operations  15.1 us (3%)
  starting transfers between devices  12.2 us (2%)
    dot_general x16, matrix products, left_apply(): jnp.einsum('kn,bnm->bkm', matrix, stacked, precision=exact_mode, preferre...  144 us
    psum x1, waiting for transfers between devices, body(): summed = lax.psum((sums[0], sums[1], sums[2]), ('trow', 'tcol'))  134 us
    dot_general x16, matrix products, right_apply(): jnp.einsum('bkn,nm->bkm', stacked, matrix, precision=exact_mode, preferre...  94.1 us
    gather x48, local copies, waits for them, and re-layouts  64.8 us
    ppermute x2, waiting for transfers between devices, padded(): before = lax.ppermute(last, axis, up)  31.1 us
    all_to_all x1, blocking collectives, body(): lax.all_to_all(outgoing.reshape(col_count * capacity, 3), 'tcol', split_a...  15.8 us
  transfers between devices with their start and end apart: 5, of which 4 were waited for; matrix products, arithmetic and copies ran while one was open for 1% of the time, Pallas kernels for 0%

commit v1 on v0

v1 whole, which is shorter than its diff:
```python
import math

import jax
import jax.numpy as jnp
import ml_dtypes
import numpy as np
from jax import lax
from jax.experimental import pallas as pl
from jax.experimental.pallas import tpu as pltpu
from jax.sharding import PartitionSpec as P

BINS = 16
FRAME = 256
HALF = 128
SLOTS = 16
TILE = 1024
PLANES = 3
BAND = 8
CHUNK = 32
PAIR = 2
EARLY = 4
VMEM_LIMIT = 62 * 1024 * 1024


def two_parts(matrix):
    high = matrix.astype(ml_dtypes.bfloat16)
    low = (matrix - high.astype(np.float64)).astype(ml_dtypes.bfloat16)
    return high, low


def tables():
    n, j = np.arange(HALF)[:, None], np.arange(HALF)[None, :]

    def real_form(steps):
        angle = 2 * np.pi * (steps % FRAME) / FRAME
        c, s = np.cos(angle) / math.sqrt(FRAME), np.sin(angle) / math.sqrt(FRAME)
        return np.block([[c, -s], [s, c]])

    even, odd = real_form(2 * n * j), real_form(n * (2 * j + 1))
    mats = np.stack([part for matrix in (even, odd, even.T, odd.T) for part in two_parts(matrix)])
    order = np.concatenate([np.arange(0, FRAME, 2), np.arange(1, FRAME, 2)])
    perm = np.zeros((FRAME, FRAME))
    perm[np.arange(FRAME), order] = 1
    perms = np.stack([perm, perm.T]).astype(ml_dtypes.bfloat16)
    freqs = ((order + HALF) % FRAME - HALF) / FRAME
    theta = 2 * np.pi * (np.arange(BINS) / BINS - 0.5)[:, None] * freqs[None, :]
    sine, cosine = np.sin(theta), np.cos(theta)
    rows = np.zeros((BINS, 16, FRAME))
    rows[:, 0], rows[:, 1], rows[:, 2], rows[:, 3] = freqs * sine, freqs * cosine, sine, cosine
    high, low = two_parts(rows)
    high[:, 4:8] = low[:, 0:4]
    scale = -2 * np.pi / FRAME
    cols = np.zeros((BINS, 8, FRAME), np.float32)
    cols[:, 0], cols[:, 1], cols[:, 2], cols[:, 3] = cosine, sine, freqs * cosine, freqs * sine
    cols[:, 4:8] = cols[:, 0:4]
    return mats, perms, high, (scale * cols).astype(np.float32)


def dot(a, b):
    return jnp.dot(a, b, preferred_element_type=jnp.float32)


def put_halves(buffer, k, rows, x):
    high = x.astype(jnp.bfloat16)
    buffer[2 * k, rows, :] = high
    buffer[2 * k + 1, rows, :] = (x - high.astype(jnp.float32)).astype(jnp.bfloat16)


def right_apply(buffer, k, mats, i):
    high, low = buffer[2 * k], buffer[2 * k + 1]
    return dot(jnp.concatenate([high, low, high], 1), jnp.concatenate([mats[2 * i], mats[2 * i], mats[2 * i + 1]], 0))


def left_apply(mats, i, buffer, k):
    high, low = buffer[2 * k], buffer[2 * k + 1]
    return dot(jnp.concatenate([mats[2 * i], mats[2 * i], mats[2 * i + 1]], 1), jnp.concatenate([high, low, high], 0))


def beside(a, b):
    return jnp.concatenate([a, b], 1)


COLS = (slice(0, HALF), slice(HALF, FRAME))


def pieces(length):
    return [(slice(r, r + CHUNK), slice(HALF + r, HALF + r + CHUNK)) for r in range(0, length, CHUNK)]


def frame_steps(window, measured, fixed, work, sums, row, col, g, row_bin, col_bin):
    probe, mats, perms, row_table, col_table = fixed
    patch, parts, middle, ordered, leaning = work
    inside = lax.broadcasted_iota(jnp.int32, (CHUNK, HALF), 1) < HALF - col
    shift = lax.rem(HALF - col, HALF)
    ordered[...] = dot(perms[0], dot(measured[...], perms[1]).astype(jnp.bfloat16)).astype(jnp.bfloat16)
    for r in range(0, FRAME, CHUNK):
        rows = slice(r, r + CHUNK)
        planes = []
        for p in range(2):
            rolled = [pltpu.roll(window[j, p, pl.ds(row + r, CHUNK), :], shift, 1) for j in range(3)]
            planes.append([jnp.where(inside, rolled[0], rolled[1]), jnp.where(inside, rolled[1], rolled[2])])
        waves = []
        for j in range(2):
            real, imag = planes[0][j], planes[1][j]
            patch[0, rows, COLS[j]] = real
            patch[1, rows, COLS[j]] = imag
            p_real, p_imag = probe[0, rows, COLS[j]], probe[1, rows, COLS[j]]
            waves.append((p_real * real - p_imag * imag, p_real * imag + p_imag * real))
        (a_real, a_imag), (b_real, b_imag) = waves
        put_halves(parts, 0, rows, beside(a_real + b_real, a_imag + b_imag))
        put_halves(parts, 1, rows, beside(a_real - b_real, a_imag - b_imag))
    yield
    for k in range(2):
        middle[k] = right_apply(parts, k, mats, k)
    yield
    for top, bottom in pieces(HALF):
        for rows, cols in ((top, COLS[0]), (bottom, COLS[1])):
            upper = beside(middle[0, top, cols], middle[1, top, cols])
            lower = beside(middle[0, bottom, cols], middle[1, bottom, cols])
            put_halves(parts, 2, rows, upper + lower)
            put_halves(parts, 3, rows, upper - lower)
    yield
    for k in range(2):
        middle[k] = left_apply(mats, 2 + k, parts, 2 + k)
    yield
    error = 0.0
    for k in range(2):
        for top, bottom in pieces(HALF):
            real, imag = middle[k, top, :], middle[k, bottom, :]
            rows = slice(HALF * k + top.start, HALF * k + top.stop)
            power = real * real + imag * imag
            gain = ordered[rows, :].astype(jnp.float32) * lax.rsqrt(power + 0.1) - 1.0
            weighted = gain * power
            error = error + jnp.sum((weighted * gain).reshape(CHUNK // 8, 8, FRAME), axis=0)
            put_halves(leaning, 0, rows, weighted)
            put_halves(parts, k, top, real * gain)
            put_halves(parts, k, bottom, imag * gain)
    sums[g, 8:16, :] = error
    yield
    for k in range(2):
        middle[k] = left_apply(mats, k, parts, k)
    moments = dot(row_table[row_bin], leaning[0]) + dot(row_table[row_bin], leaning[1])
    sums[g, 0:8, :] = moments[:8] * col_table[col_bin]
    yield
    for top, bottom in pieces(HALF):
        for k, cols in enumerate(COLS):
            even = beside(middle[0, top, cols], middle[0, bottom, cols])
            odd = beside(middle[1, top, cols], middle[1, bottom, cols])
            put_halves(parts, 2 + k, top, even + odd)
            put_halves(parts, 2 + k, bottom, even - odd)
    yield
    for k in range(2):
        middle[k] = right_apply(parts, 2 + k, mats, 2 + k)


def add_terms(works, totals):
    for r in range(0, FRAME, CHUNK):
        rows = slice(r, r + CHUNK)
        for j, cols in enumerate(COLS):
            added = [totals[p, rows, cols] for p in range(PLANES)]
            for patch, _, middle, _, _ in works:
                even, odd = middle[0, rows, :], middle[1, rows, :]
                chi = even + odd if j == 0 else even - odd
                chi_real, chi_imag = chi[:, :HALF], chi[:, HALF:]
                real, imag = patch[0, rows, cols], patch[1, rows, cols]
                added[0] += real * chi_real + imag * chi_imag
                added[1] += real * chi_imag - imag * chi_real
                added[2] += real * real + imag * imag
            for p in range(PLANES):
                totals[p, rows, cols] = added[p]


def spread(core, destinations, all_sums, all_totals, keep, send, records, line, held, taken):
    bands = FRAME // BAND // 2
    for out, half in ((keep, core), (send, 1 - core)):
        for k in range(bands):
            rows = pl.ds(pl.multiple_of(half * HALF + BAND * k, BAND), BAND)
            for p in range(PLANES):
                out[k, BAND * p : BAND * (p + 1), :] = sum(totals[p, rows, :] for totals in all_totals)
    sums = sum(part[...] for part in all_sums)
    grad_y = jnp.sum(sums[:, 0, :] + sums[:, 1, :] + sums[:, 4, :] + sums[:, 5, :], axis=1, keepdims=True)
    grad_x = jnp.sum(sums[:, 2, :] + sums[:, 3, :] + sums[:, 6, :] + sums[:, 7, :], axis=1, keepdims=True)
    error = jnp.sum(jnp.sum(sums[:, 8:16, :], axis=1), axis=1, keepdims=True) / (FRAME * FRAME)
    lane = lax.broadcasted_iota(jnp.int32, (SLOTS, HALF), 1)
    line[...] = jnp.where(lane == 0, grad_y, jnp.where(lane == 1, grad_x, jnp.where(lane == 2, error, 0.0)))
    held[...] = jnp.zeros_like(held)

    for k in range(2 * bands):
        taken[k] = 0
    for g in range(SLOTS):
        target = destinations[0, g]
        rank = taken[target]
        taken[target] = rank + 1
        held[target, pl.ds(rank, 1), :] = line[g : g + 1, :]
    for k in range(bands):
        records[k] = beside(held[2 * k], held[2 * k + 1])


def frames_kernel(stage):
    first, last = stage == 0, stage == 2
    row_edge = last
    n_strips = 6 if last else 0 if first else 2

    def kernel(*refs):
        refs = list(refs)

        def take(count):
            taken = refs[:count]
            del refs[:count]
            return taken

        positions, bins, counts = take(3)
        if not first:
            (odds,) = take(1)
        if last:
            (destinations,) = take(1)
        measured, tile = take(2)
        tables_in = take(5)
        strips = take(n_strips)
        if last:
            earlier = take(4)
            keep, send, records, totals, sums, line, placed, taken = take(8)
            held = take(4)
        else:
            totals, sums = take(2)
        window, buffer, todo, sems, table_sems = take(5)
        fixed = take(5)
        work = refs

        def choose(g, carry):
            n, seen = carry
            r, c = positions[0, g], positions[1, g]
            row_out = (r < HALF) | (r >= TILE - HALF)
            wanted = (g < counts[0]) & (row_out == row_edge)
            if not row_edge:
                free = wanted & (c >= HALF) & (c < TILE - HALF)
                early = free & (seen < EARLY)
                seen = seen + free.astype(jnp.int32)
                wanted = early if first else wanted & jnp.logical_not(early)
            todo[n] = g
            return n + wanted.astype(jnp.int32), seen

        n, _ = lax.fori_loop(0, SLOTS, choose, (jnp.int32(0), jnp.int32(0)), unroll=True)

        def copies(i):
            g = todo[i]
            slot = lax.rem(i, 2 * PAIR)
            r, c = positions[0, g], positions[1, g]
            on_top, on_left, on_right = r < HALF, c < HALF, c >= TILE - HALF
            off_left, off_right = c >= HALF, c < TILE - HALF
            if not first:
                col_side = [on_left == (odds[0] == 1), on_left != (odds[0] == 1)]
                row_side = [on_top == (odds[1] == 1), on_top != (odds[1] == 1)]
            left = (c // HALF - 1) * HALF

            def option(cond, ref, row, col, length, dst, j, sem):
                source = ref.at[:, pl.ds(row, length), pl.ds(pl.multiple_of(col, HALF), HALF)]
                return cond, source, window.at[slot, j, :, pl.ds(dst, length)], sems.at[slot, sem]

            if row_edge:
                mid_row = pl.multiple_of(jnp.where(on_top, 0, TILE - 2 * HALF), HALF)
                mid_dst = pl.multiple_of(jnp.where(on_top, HALF, 0), HALF)
                end_dst = pl.multiple_of(jnp.where(on_top, 0, 2 * HALF), HALF)
                length = 2 * HALF
            else:
                mid_row, mid_dst, length = pl.multiple_of((r // 8) * 8 - HALF, 8), 0, FRAME + 8
            found = []
            for j in range(3):
                col = jnp.clip(left + HALF * j, 0, TILE - HALF)
                if first or j == 1:
                    found.append([option(None, tile, mid_row, col, length, mid_dst, j, j)])
                else:
                    beyond, within = (on_left, off_left) if j == 0 else (on_right, off_right)
                    options = [option(within, tile, mid_row, col, length, mid_dst, j, j)]
                    for w in range(2):
                        options.append(option(beyond & col_side[w], strips[w], mid_row, 0, length, mid_dst, j, j))
                    found.append(options)
                if row_edge:
                    options = []
                    for v in range(2):
                        here = row_side[v]
                        if j == 1:
                            options.append(option(here, strips[2 + v], 0, col, HALF, end_dst, j, 3 + j))
                        else:
                            options.append(option(here & within, strips[2 + v], 0, col, HALF, end_dst, j, 3 + j))
                            for w in range(2):
                                corner = strips[4 + v].at[w]
                                options.append(option(here & beyond & col_side[w], corner, 0, 0, HALF, end_dst, j, 3 + j))
                    found.append(options)
            found.append([(None, measured.at[g], buffer.at[slot], sems.at[slot, 6])])
            return found

        def start(i):
            @pl.when(i < n)
            def _():
                for options in copies(i):
                    for cond, *ends in options:
                        if cond is None:
                            pltpu.make_async_copy(*ends).start()
                        else:
                            pl.when(cond)(pltpu.make_async_copy(*ends).start)

        for u in range(PAIR):
            start(u)
        loads = [pltpu.make_async_copy(src, dst, table_sems.at[k]) for k, (src, dst) in enumerate(zip(tables_in, fixed))]
        for load in loads:
            load.start()
        if last:
            recalls = [pltpu.make_async_copy(src, dst, table_sems.at[5 + k]) for k, (src, dst) in enumerate(zip(earlier, held))]
            for recall in recalls:
                recall.start()
        totals[...] = jnp.zeros_like(totals)
        sums[...] = jnp.zeros_like(sums)
        for load in loads:
            load.wait()

        def together(i, count):
            for u in range(count):
                for options in copies(PAIR * i + u):
                    pltpu.make_async_copy(*options[0][1:]).wait()
            works, runs = [], []
            for u in range(count):
                k = PAIR * i + u
                g, slot = todo[k], lax.rem(k, 2 * PAIR)
                r, c = positions[0, g], positions[1, g]
                works.append([ref.at[u] for ref in work])
                row = jnp.where(r < HALF, r, r - (TILE - HALF)) if row_edge else lax.rem(r, 8)
                runs.append(
                    frame_steps(
                        window.at[slot], buffer.at[slot], fixed, works[u], sums, row, lax.rem(c, HALF), g, bins[0, g], bins[1, g]
                    )
                )
            while runs:
                runs = [run for run in runs if next(run, runs) is None]
            add_terms(works, totals)

        def step(i, _):
            for u in range(PAIR):
                start(PAIR * (i + 1) + u)
            together(i, PAIR)
            return 0

        full = n // PAIR
        lax.fori_loop(0, full, step, 0)
        for count in range(1, PAIR):
            pl.when(n - PAIR * full == count)(lambda: together(full, count))
        if last:
            for recall in recalls:
                recall.wait()
            spread(odds[0], destinations, (sums, held[1], held[3]), (totals, held[0], held[2]), keep, send, records, line, placed, taken)

    return kernel


SMEM = pl.BlockSpec(memory_space=pltpu.SMEM)
VMEM = pl.BlockSpec(memory_space=pltpu.VMEM)
HBM = pl.BlockSpec(memory_space=pltpu.HBM)
ANY = pl.BlockSpec(memory_space=pl.ANY)


def f32(*shape):
    return jax.ShapeDtypeStruct(shape, jnp.float32)


def frames_call(stage, scalars, sources, fixed, strips=(), earlier=(), extra=()):
    last = stage == 2
    bands = FRAME // BAND // 2
    totals_shape, sums_shape = (PLANES, FRAME, FRAME), (SLOTS, 16, FRAME)
    scratch = []
    if last:
        out_shape = [f32(bands, PLANES * BAND, FRAME)] * 2 + [f32(bands, BAND, FRAME)]
        scratch = [pltpu.VMEM(totals_shape, jnp.float32), pltpu.VMEM(sums_shape, jnp.float32), pltpu.VMEM((SLOTS, HALF), jnp.float32)]
        scratch += [pltpu.VMEM((2 * bands, BAND, HALF), jnp.float32), pltpu.SMEM((2 * bands,), jnp.int32)]
        scratch += [pltpu.VMEM(shape, jnp.float32) for shape in (totals_shape, sums_shape) * 2]
    else:
        out_shape = [f32(*totals_shape), f32(*sums_shape)]
    rows = 3 * HALF if last else FRAME + 8
    scratch += [
        pltpu.VMEM((2 * PAIR, 3, 2, rows, HALF), jnp.float32),
        pltpu.VMEM((2 * PAIR, FRAME, FRAME), jnp.bfloat16),
        pltpu.SMEM((SLOTS + 1,), jnp.int32),
        pltpu.SemaphoreType.DMA((2 * PAIR, 7)),
        pltpu.SemaphoreType.DMA((9,)),
        *(pltpu.VMEM(t.shape, t.dtype) for t in fixed),
        pltpu.VMEM((PAIR, 2, FRAME, FRAME), jnp.float32),
        pltpu.VMEM((PAIR, 8, FRAME, FRAME), jnp.bfloat16),
        pltpu.VMEM((PAIR, 2, FRAME, FRAME), jnp.float32),
        pltpu.VMEM((PAIR, FRAME, FRAME), jnp.bfloat16),
        pltpu.VMEM((PAIR, 2, FRAME, FRAME), jnp.bfloat16),
    ]
    scalars = [*scalars, *extra]
    return pl.pallas_call(
        frames_kernel(stage),
        in_specs=[SMEM] * len(scalars) + [ANY] * (7 + len(strips) + len(earlier)),
        out_specs=[VMEM] * len(out_shape),
        out_shape=out_shape,
        scratch_shapes=scratch,
        compiler_params=pltpu.CompilerParams(vmem_limit_bytes=VMEM_LIMIT),
        cost_estimate=pl.CostEstimate(flops=int(8e9), bytes_accessed=int(2e7), transcendentals=0),
    )(*scalars, *sources, *fixed, *strips, *earlier)


def strips_kernel(odds, tile, *refs):
    outs, held, sems = refs[:4], refs[4:8], refs[8]
    inner = TILE - HALF
    cols, rows = [[(pl.multiple_of(jnp.where(odds[k] == side, inner, 0), HALF), HALF) for side in (0, 1)] for k in (0, 1)]
    whole = (0, TILE)
    boxes = [(r, whole) for r in rows] + [(whole, c) for c in cols]
    loads = [
        pltpu.make_async_copy(tile.at[:, pl.ds(*r), pl.ds(*c)], here, sems.at[0, k])
        for k, ((r, c), here) in enumerate(zip(boxes, held))
    ]
    stores = [pltpu.make_async_copy(here, out, sems.at[1, k]) for k, (here, out) in enumerate(zip(held, outs))]
    for load in loads:
        load.start()
    for load, store in zip(loads, stores):
        load.wait()
        store.start()
    for store in stores:
        store.wait()


def strips_call(odds, tile):
    shapes = [(2, HALF, TILE)] * 2 + [(2, TILE, HALF)] * 2
    return pl.pallas_call(
        strips_kernel,
        in_specs=[SMEM, ANY],
        out_specs=[ANY] * 4,
        out_shape=[f32(*shape) for shape in shapes],
        scratch_shapes=[pltpu.VMEM(shape, jnp.float32) for shape in shapes] + [pltpu.SemaphoreType.DMA((2, 4))],
        compiler_params=pltpu.CompilerParams(vmem_limit_bytes=VMEM_LIMIT),
    )(odds, tile)


def body(object_slab, probe_field, amplitudes, positions, shift_bins, destinations, frame_counts):
    cols = lax.axis_size("tcol")

    def swapped(array, axis, side):
        n = lax.axis_size(axis)
        return lax.ppermute(array, axis, [pair for i in range(side, n - 1, 2) for pair in ((i, i + 1), (i + 1, i))])

    def across(array, axis, mask):
        return lax.ppermute(array, axis, [(i, i ^ mask) for i in range(lax.axis_size(axis))])

    def dealt(array):
        groups = [list(range(c, cols, 2)) for c in range(2)]
        return lax.all_to_all(array, "tcol", 0, 0, axis_index_groups=groups, tiled=True)

    odds = jnp.stack([lax.axis_index("tcol") % 2, lax.axis_index("trow") % 2]).astype(jnp.int32)
    sent = strips_call(odds, object_slab)
    rows = [swapped(sent[side], "trow", side) for side in range(2)]
    sides = [swapped(sent[2 + side], "tcol", side) for side in range(2)]
    scalars = (positions.T, shift_bins.T, frame_counts)
    sources = (amplitudes, object_slab)
    fixed = (probe_field, *(jnp.asarray(t) for t in tables()))
    begun = frames_call(0, scalars, sources, fixed)
    sides, begun = lax.optimization_barrier((sides, begun))
    both = jnp.stack(sides)
    low, high = both[:, :, TILE - HALF :], both[:, :, :HALF]
    corners = [swapped(jnp.where(odds[1] == side, low, high), "trow", side) for side in range(2)]
    between = frames_call(1, scalars, sources, fixed, sides, extra=(odds,))
    keep, send, records = frames_call(
        2, scalars, sources, fixed, (*sides, *rows, *corners), (*begun, *between), (odds, destinations.T)
    )
    summed = jnp.sum(dealt(keep + across(send, "tcol", 1)), axis=0)
    for mask in (1, 3):
        summed = summed + across(summed, "trow", mask)
    root = lax.rsqrt(summed[2 * BAND :] + 1.0)
    step = summed[: 2 * BAND] * jnp.concatenate([root, root], 0)
    out = jnp.concatenate([jnp.broadcast_to(step, (FRAME // BAND // 2, 2 * BAND, FRAME)), records], 1)
    mine = dealt(out)
    theirs = across(mine, "tcol", 1)
    odd = odds[0] == 1
    both = jnp.stack([jnp.where(odd, theirs, mine), jnp.where(odd, mine, theirs)])
    bands = FRAME // BAND // 2
    step = both[:, :, : 2 * BAND].reshape(2, bands, 2, BAND, FRAME)
    probe_step = jnp.transpose(step, (2, 0, 1, 3, 4)).reshape(2, FRAME, FRAME)
    record = both[:, :, 2 * BAND : 2 * BAND + 2]
    record = jnp.where(odd, record[..., HALF : HALF + 3], record[..., 0:3])
    return probe_step, jnp.transpose(record, (1, 0, 2, 3)).reshape(4 * bands, 3)


def solution(mesh):
    in_specs = (
        P(None, "trow", "tcol"),
        P(),
        P(("trow", "tcol"), None, None),
        P(("trow", "tcol"), None),
        P(("trow", "tcol"), None),
        P(("trow", "tcol"), None),
        P(("trow", "tcol")),
    )
    out_specs = (P(), P(("trow", "tcol"), None))
    return jax.shard_map(body, mesh=mesh, in_specs=in_specs, out_specs=out_specs, check_vma=False)
```

time: 555 us -> 103 us (0.19)
  matrix products: 238 us -> 0 us
  waiting for transfers between devices: 170 us -> 12.2 us
  local copies, waits for them, and re-layouts: 80.3 us -> 2.61 us
  Pallas kernels: 0 us -> 26.4 us
  blocking collectives: 15.8 us -> 33.7 us
  between operations: 15.1 us -> 1.43 us
  other arithmetic: 16.7 us -> 4.04 us
  starting transfers between devices: 12.2 us -> 20.8 us
    dot_general x33 -> x0, matrix products: 238 us -> none  [the longest x16 144 us: left_apply(): jnp.einsum('kn,bnm->bkm', matrix, stacked, precision=exact_mode, preferre...]
    psum x1 -> x0, waiting for transfers between devices: 134 us -> none  [body(): summed = lax.psum((sums[0], sums[1], sums[2]), ('trow', 'tcol'))]
    gather x48 -> x0, local copies, waits for them, and re-layouts: 64.8 us -> none
    pallas_call x0 -> x4, Pallas kernels: none -> 26.4 us  [the longest x3 22.4 us: frames_call(): pl.pallas_call(frames_kernel(stage), in_specs=[SMEM] * len(scalars) + [AN...]
    ppermute x4 -> x10, waiting for transfers between devices: 35.5 us -> 12.2 us  [the longest x6 6.27 us: swapped(): lax.ppermute(array, axis, [pair for i in range(side, n - 1, 2) for pair i...]
    all_to_all x1 -> x2, blocking collectives: 15.8 us -> 33.7 us  [dealt(): lax.all_to_all(array, 'tcol', 0, 0, axis_index_groups=groups, tiled=True)]
    concatenate x3 -> x1, other arithmetic: 10.1 us -> 0.93 us  [body(): jnp.concatenate([jnp.broadcast_to(step, (FRAME // BAND // 2, 2 * BAND, FR...]
    ppermute x4 -> x10, starting transfers between devices: 12.2 us -> 20.8 us  [the longest x6 10.9 us: swapped(): lax.ppermute(array, axis, [pair for i in range(side, n - 1, 2) for pair i...]
  transfers between devices with their start and end apart: 5 -> 10, of which waited for: 4 -> 7; matrix products, arithmetic and copies ran while one was open for 1% -> 1% of each run, Pallas kernels for 0% -> 15%
where the time goes in v1:
time: 103 us; the launch traced here: 101 us
  blocking collectives  33.7 us (33%)
  Pallas kernels  26.4 us (26%)
  starting transfers between devices  20.8 us (20%)
  waiting for transfers between devices  12.2 us (12%)
  other arithmetic  4.04 us (4%)
  local copies, waits for them, and re-layouts  2.61 us (3%)
  between operations  1.43 us (1%)
    all_to_all x2, blocking collectives, dealt(): lax.all_to_all(array, 'tcol', 0, 0, axis_index_groups=groups, tiled=True)  33.7 us
    pallas_call x3, Pallas kernels, frames_call(): pl.pallas_call(frames_kernel(stage), in_specs=[SMEM] * len(scalars) + [AN...  22.4 us
    ppermute x6, starting transfers between devices, swapped(): lax.ppermute(array, axis, [pair for i in range(side, n - 1, 2) for pair i...  10.9 us
    ppermute x4, starting transfers between devices, across(): lax.ppermute(array, axis, [(i, i ^ mask) for i in range(lax.axis_size(axi...  9.85 us
    ppermute x6, waiting for transfers between devices, swapped(): lax.ppermute(array, axis, [pair for i in range(side, n - 1, 2) for pair i...  6.27 us
    ppermute x4, waiting for transfers between devices, across(): lax.ppermute(array, axis, [(i, i ^ mask) for i in range(lax.axis_size(axi...  5.9 us
    pallas_call x1, Pallas kernels, strips_call(): pl.pallas_call(strips_kernel, in_specs=[SMEM, ANY], out_specs=[ANY] * 4,...  4.07 us
  transfers between devices with their start and end apart: 10, of which 7 were waited for; matrix products, arithmetic and copies ran while one was open for 1% of the time, Pallas kernels for 15%

profile of v1, /device:TPU:1, one launch (start us, length us, event | category | flops | bytes accessed | tf_op | source)
XLA Modules:
  0.0 101.1 jit_solution(10734329872764048891)
XLA Ops:
  0.6 0.6 pad_add_fusion.odds.refs_3_
  1.3 4.1 %shard_map.122 = (f32[2,128,1024]{2,1,0:T(8,128)}, f32[2,128,1024]{2,1,0:T(8,128)}, f32[2,1024,128]{2,1,0:T(8,128)}, f32[2,1024,128]{2,1,0:T(8,128)}) custom-call(s32[2]{0:T(128)} %pad_add_fusion.odds.refs_3_, f32[2,1024,1024]{2,1,0:T(8,128)} %refs_6_.4), custom_call_target="tpu_custom_call" | custom-call | tf_op jit(solution)/shard_map/pallas_call | solution.py:425
  5.4 1.5 %collective-permute-start = (f32[2,1024,128]{2,1,0:T(8,128)}, f32[2,1024,128]{2,1,0:T(8,128)S(1)}, u32[]{:S(2)}, u32[]{:S(2)}) collective-permute-start(f32[2,1024,128]{2,1,0:T(8,128)} %get-tuple-element.17), channel_id=1, source_target_pairs={{0,1},{1,0},{2,3},{3,2},{4,5},{5,4},{6,7},{7,6},{8,9},{9,8},{10,11... | collective-permute-start | bytes 3145736 | tf_op jit(solution)/shard_map/ppermute | solution.py:440
  6.9 3.1 %collective-permute-start.1 = (f32[2,1024,128]{2,1,0:T(8,128)}, f32[2,1024,128]{2,1,0:T(8,128)}, u32[]{:S(2)}, u32[]{:S(2)}) collective-permute-start(f32[2,1024,128]{2,1,0:T(8,128)} %get-tuple-element.18), channel_id=1, source_target_pairs={{1,2},{2,1},{3,4},{4,3},{5,6},{6,5},{7,8},{8,7},{9,10},{10,9},{11,... | collective-permute-start | bytes 3145736 | tf_op jit(solution)/shard_map/ppermute | solution.py:440
  10.0 1.7 %collective-permute-start.2 = (f32[2,128,1024]{2,1,0:T(8,128)}, f32[2,128,1024]{2,1,0:T(8,128)}, u32[]{:S(2)}, u32[]{:S(2)}) collective-permute-start(f32[2,128,1024]{2,1,0:T(8,128)} %get-tuple-element.23), channel_id=1, source_target_pairs={{0,32},{32,0},{64,96},{96,64},{1,33},{33,1},{65,97},{97,65},{2,34}... | collective-permute-start | bytes 3145736 | tf_op jit(solution)/shard_map/ppermute | solution.py:440
  11.7 1.6 %collective-permute-start.3 = (f32[2,128,1024]{2,1,0:T(8,128)}, f32[2,128,1024]{2,1,0:T(8,128)}, u32[]{:S(2)}, u32[]{:S(2)}) collective-permute-start(f32[2,128,1024]{2,1,0:T(8,128)} %get-tuple-element.24), channel_id=1, source_target_pairs={{32,64},{64,32},{33,65},{65,33},{34,66},{66,34},{35,67},{67,35},{3... | collective-permute-start | bytes 3145736 | tf_op jit(solution)/shard_map/ppermute | solution.py:440
  14.0 9.4 %shard_map.123 = (f32[3,256,256]{2,1,0:T(8,128)}, f32[16,16,256]{2,1,0:T(8,128)}) custom-call(s32[2,16]{1,0:T(2,128)} %bitcast.22, s32[2,16]{1,0:T(2,128)} %bitcast.25, s32[1]{0:T(128)S(6)} %copy.19.refs_2_, bf16[16,256,256]{2,1,0:T(8,128)(2,1)} %refs_5_.5, f32[2,1024,1024]{2,1,0:T(8,128)} %refs_6_.4, f32[2,256,256]{2,1,0:T(8,128)} %refs_7_.3, ...), custom_call_target="tpu_custom_call" | custom-call | flops 8000000000 | bytes 20000000 | tf_op jit(solution)/shard_map/pallas_call | solution.py:392
  23.4 0.2 collective-permute-done.1.refs_12_.refs_13_
  23.6 1.2 %broadcast_select_fusion = (f32[2,2,128,128]{3,2,1,0:T(8,128)S(1)}, f32[2,2,128,128]{3,2,1,0:T(8,128)S(1)}, f32[2,2,128,128]{3,2,1,0:T(8,128)S(1)}) fusion(pred[]{:T(512)S(6)} %eq.14, f32[1,2,1024,128]{3,2,1,0:T(8,128)} %bitcast.6, f32[1,2,1024,128]{3,2,1,0:T(8,128)S(1)} %bitcast.20), kind=kLoop, calls=%fused_computation.11 | loop fusion | flops 196608 | bytes 2883585 | tf_op jit(solution)/shard_map/jit(_where)/select_n | solution.py:460
  24.8 1.6 %collective-permute-start.4 = (f32[2,2,128,128]{3,2,1,0:T(8,128)S(1)}, f32[2,2,128,128]{3,2,1,0:T(8,128)S(1)}, u32[]{:S(2)}, u32[]{:S(2)}) collective-permute-start(f32[2,2,128,128]{3,2,1,0:T(8,128)S(1)} %broadcast_select_fusion.1), channel_id=1, source_target_pairs={{0,32},{32,0},{64,96},{96,64},{1,33},{33,1},{65,97},{97,65},{2,34}... | collective-permute-start | bytes 786440 | tf_op jit(solution)/shard_map/ppermute | solution.py:440
  26.4 1.4 %collective-permute-start.5 = (f32[2,2,128,128]{3,2,1,0:T(8,128)S(1)}, f32[2,2,128,128]{3,2,1,0:T(8,128)}, u32[]{:S(2)}, u32[]{:S(2)}) collective-permute-start(f32[2,2,128,128]{3,2,1,0:T(8,128)S(1)} %get-tuple-element.32), channel_id=1, source_target_pairs={{32,64},{64,32},{33,65},{65,33},{34,66},{66,34},{35,67},{67,35},{3... | collective-permute-start | bytes 786440 | tf_op jit(solution)/shard_map/ppermute | solution.py:440
  27.8 5.8 %shard_map.124 = (f32[3,256,256]{2,1,0:T(8,128)}, f32[16,16,256]{2,1,0:T(8,128)}) custom-call(s32[2,16]{1,0:T(2,128)} %bitcast.23, s32[2,16]{1,0:T(2,128)} %bitcast.26, s32[1]{0:T(128)S(6)} %copy.19.refs_2_, s32[2]{0:T(128)} %pad_add_fusion.odds.refs_3_, bf16[16,256,256]{2,1,0:T(8,128)(2,1)} %refs_5_.5, f32[2,1024,1024]{2,1,0:T(8,128)} %refs_6_.4, ...), custom_call_target="tpu_custom_call" | custom-call | flops 8000000000 | bytes 20000000 | tf_op jit(solution)/shard_map/pallas_call | solution.py:392
  33.6 2.0 %collective-permute-done.2.refs_14_ = f32[2,128,1024]{2,1,0:T(8,128)} collective-permute-done((f32[2,128,1024]{2,1,0:T(8,128)}, f32[2,128,1024]{2,1,0:T(8,128)}, u32[]{:S(2)}, u32[]{:S(2)}) %collective-permute-start.2) | collective-permute-done | bytes 1048608 | tf_op jit(solution)/shard_map/ppermute | solution.py:440
  35.7 4.0 %collective-permute-done.4.refs_16_ = f32[2,2,128,128]{3,2,1,0:T(8,128)S(1)} collective-permute-done((f32[2,2,128,128]{3,2,1,0:T(8,128)S(1)}, f32[2,2,128,128]{3,2,1,0:T(8,128)S(1)}, u32[]{:S(2)}, u32[]{:S(2)}) %collective-permute-start.4) | collective-permute-done | bytes 262176 | tf_op jit(solution)/shard_map/ppermute | solution.py:440
  39.7 0.7 copy-done.1
  40.4 7.2 %shard_map.125 = (f32[16,24,256]{2,1,0:T(8,128)}, f32[16,24,256]{2,1,0:T(8,128)}, f32[16,8,256]{2,1,0:T(8,128)}) custom-call(s32[2,16]{1,0:T(2,128)} %bitcast.24, s32[2,16]{1,0:T(2,128)} %bitcast.27, s32[1]{0:T(128)S(6)} %copy.19.refs_2_, s32[2]{0:T(128)} %pad_add_fusion.odds.refs_3_, s32[1,16]{1,0:T(1,128)} %bitcast.28, bf16[16,256,256]{2,1,0:T(8,128)(2,1)} %refs_5_.5, ...), custom_call_target="tpu_custom_call" | custom-call | flops 8000000000 | bytes 20000000 | tf_op jit(solution)/shard_map/pallas_call | solution.py:392
  47.6 0.1 collective-permute-start.6
  47.7 1.9 %collective-permute-done.6 = f32[16,24,256]{2,1,0:T(8,128)S(1)} collective-permute-done((f32[16,24,256]{2,1,0:T(8,128)}, f32[16,24,256]{2,1,0:T(8,128)S(1)}, u32[]{:S(2)}, u32[]{:S(2)}) %collective-permute-start.6) | collective-permute-done | bytes 393248 | tf_op jit(solution)/shard_map/ppermute | solution.py:443
  49.6 1.0 %add.24 = f32[16,24,256]{2,1,0:T(8,128)S(1)} add(f32[16,24,256]{2,1,0:T(8,128)} %get-tuple-element.29, f32[16,24,256]{2,1,0:T(8,128)S(1)} %collective-permute-done.6) | non-fusion elementwise | flops 98304 | bytes 1179648 | tf_op jit(solution)/shard_map/add | solution.py:465
  50.7 22.5 %all_to_all.10 = f32[16,24,256]{2,1,0:T(8,128)S(1)} all-to-all(f32[16,24,256]{2,1,0:T(8,128)S(1)} %add.24), channel_id=1, replica_groups={{0,2,4,6,8,10,12,14,16,18,20,22,24,26,28,30},{1,3,5,7,9,11,13,15,17,19,..., dimensions={0} | all-to-all | bytes 786432 | tf_op jit(solution)/shard_map/all_to_all | solution.py:447
  73.2 2.6 %collective-permute-start.7 = (f32[24,256]{1,0:T(8,128)S(1)}, f32[24,256]{1,0:T(8,128)S(1)}, u32[]{:S(2)}, u32[]{:S(2)}) collective-permute-start(f32[24,256]{1,0:T(8,128)S(1)} %reduce_sum.9), channel_id=1, source_target_pairs={{0,32},{32,0},{64,96},{96,64},{1,33},{33,1},{65,97},{97,65},{2,34}... | collective-permute-start | bytes 73736 | tf_op jit(solution)/shard_map/ppermute | solution.py:443
  75.8 1.2 %collective-permute-done.7 = f32[24,256]{1,0:T(8,128)S(1)} collective-permute-done((f32[24,256]{1,0:T(8,128)S(1)}, f32[24,256]{1,0:T(8,128)S(1)}, u32[]{:S(2)}, u32[]{:S(2)}) %collective-permute-start.7) | collective-permute-done | bytes 24608 | tf_op jit(solution)/shard_map/ppermute | solution.py:443
  77.0 2.5 %collective-permute-start.8 = (f32[24,256]{1,0:T(8,128)S(1)}, f32[24,256]{1,0:T(8,128)S(1)}, u32[]{:S(2)}, u32[]{:S(2)}) collective-permute-start(f32[24,256]{1,0:T(8,128)S(1)} %add.25), channel_id=1, source_target_pairs={{0,96},{32,64},{64,32},{96,0},{1,97},{33,65},{65,33},{97,1},{2,98}... | collective-permute-start | bytes 73736 | tf_op jit(solution)/shard_map/ppermute | solution.py:443
  79.5 1.4 %collective-permute-done.8 = f32[24,256]{1,0:T(8,128)S(1)} collective-permute-done((f32[24,256]{1,0:T(8,128)S(1)}, f32[24,256]{1,0:T(8,128)S(1)}, u32[]{:S(2)}, u32[]{:S(2)}) %collective-permute-start.8) | collective-permute-done | bytes 24608 | tf_op jit(solution)/shard_map/ppermute | solution.py:443
  81.0 0.9 pad_maximum_fusion
  81.9 11.2 %all_to_all.11 = f32[16,24,256]{2,1,0:T(8,128)S(1)} all-to-all(f32[16,24,256]{2,1,0:T(8,128)S(1)} %pad_maximum_fusion), channel_id=1, replica_groups={{0,2,4,6,8,10,12,14,16,18,20,22,24,26,28,30},{1,3,5,7,9,11,13,15,17,19,..., dimensions={0} | all-to-all | bytes 786432 | tf_op jit(solution)/shard_map/all_to_all | solution.py:447
  93.1 4.7 %collective-permute-start.9 = (f32[16,24,256]{2,1,0:T(8,128)S(1)}, f32[16,24,256]{2,1,0:T(8,128)S(1)}, u32[]{:S(2)}, u32[]{:S(2)}) collective-permute-start(f32[16,24,256]{2,1,0:T(8,128)S(1)} %all_to_all.11), channel_id=1, source_target_pairs={{0,1},{1,0},{2,3},{3,2},{4,5},{5,4},{6,7},{7,6},{8,9},{9,8},{10,11... | collective-permute-start | bytes 1179656 | tf_op jit(solution)/shard_map/ppermute | solution.py:443
  97.7 1.3 %collective-permute-done.9 = f32[16,24,256]{2,1,0:T(8,128)S(1)} collective-permute-done((f32[16,24,256]{2,1,0:T(8,128)S(1)}, f32[16,24,256]{2,1,0:T(8,128)S(1)}, u32[]{:S(2)}, u32[]{:S(2)}) %collective-permute-start.9) | collective-permute-done | bytes 393248 | tf_op jit(solution)/shard_map/ppermute | solution.py:443
  99.1 0.1 fusion.1
  99.2 0.8 copy.17
  100.1 0.3 copy.18
  100.4 0.7 reshape.15
  (15 shorter events, 0.2 us)
Async XLA Ops:
  5.4 18.0 %collective-permute-start = (f32[2,1024,128]{2,1,0:T(8,128)}, f32[2,1024,128]{2,1,0:T(8,128)S(1)}, u32[]{:S(2)}, u32[]{:S(2)}) collective-permute-start(f32[2,1024,128]{2,1,0:T(8,128)} %get-tuple-element.17), channel_id=1, source_target_pairs={{0,1},{1,0},{2,3},{3,2},{4,5},{5,4},{6,7},{7,6},{8,9},{9,8},{10,11... | collective-permute-start | bytes 3145736 | tf_op jit(solution)/shard_map/ppermute | solution.py:440
  6.9 16.7 %collective-permute-start.1 = (f32[2,1024,128]{2,1,0:T(8,128)}, f32[2,1024,128]{2,1,0:T(8,128)}, u32[]{:S(2)}, u32[]{:S(2)}) collective-permute-start(f32[2,1024,128]{2,1,0:T(8,128)} %get-tuple-element.18), channel_id=1, source_target_pairs={{1,2},{2,1},{3,4},{4,3},{5,6},{6,5},{7,8},{8,7},{9,10},{10,9},{11,... | collective-permute-start | bytes 3145736 | tf_op jit(solution)/shard_map/ppermute | solution.py:440
  10.0 25.7 %collective-permute-start.2 = (f32[2,128,1024]{2,1,0:T(8,128)}, f32[2,128,1024]{2,1,0:T(8,128)}, u32[]{:S(2)}, u32[]{:S(2)}) collective-permute-start(f32[2,128,1024]{2,1,0:T(8,128)} %get-tuple-element.23), channel_id=1, source_target_pairs={{0,32},{32,0},{64,96},{96,64},{1,33},{33,1},{65,97},{97,65},{2,34}... | collective-permute-start | bytes 3145736 | tf_op jit(solution)/shard_map/ppermute | solution.py:440
  11.7 24.0 %collective-permute-start.3 = (f32[2,128,1024]{2,1,0:T(8,128)}, f32[2,128,1024]{2,1,0:T(8,128)}, u32[]{:S(2)}, u32[]{:S(2)}) collective-permute-start(f32[2,128,1024]{2,1,0:T(8,128)} %get-tuple-element.24), channel_id=1, source_target_pairs={{32,64},{64,32},{33,65},{65,33},{34,66},{66,34},{35,67},{67,35},{3... | collective-permute-start | bytes 3145736 | tf_op jit(solution)/shard_map/ppermute | solution.py:440
  23.4 4.4 %copy-start = (f32[2,1024,128]{2,1,0:T(8,128)}, f32[2,1024,128]{2,1,0:T(8,128)S(1)}, u32[]{:S(2)}) copy-start(f32[2,1024,128]{2,1,0:T(8,128)S(1)} %collective-permute-done.refs_11_.refs_12_) | copy-start | bytes 3145732
  24.8 14.9 %collective-permute-start.4 = (f32[2,2,128,128]{3,2,1,0:T(8,128)S(1)}, f32[2,2,128,128]{3,2,1,0:T(8,128)S(1)}, u32[]{:S(2)}, u32[]{:S(2)}) collective-permute-start(f32[2,2,128,128]{3,2,1,0:T(8,128)S(1)} %broadcast_select_fusion.1), channel_id=1, source_target_pairs={{0,32},{32,0},{64,96},{96,64},{1,33},{33,1},{65,97},{97,65},{2,34}... | collective-permute-start | bytes 786440 | tf_op jit(solution)/shard_map/ppermute | solution.py:440
  26.4 13.3 %collective-permute-start.5 = (f32[2,2,128,128]{3,2,1,0:T(8,128)S(1)}, f32[2,2,128,128]{3,2,1,0:T(8,128)}, u32[]{:S(2)}, u32[]{:S(2)}) collective-permute-start(f32[2,2,128,128]{3,2,1,0:T(8,128)S(1)} %get-tuple-element.32), channel_id=1, source_target_pairs={{32,64},{64,32},{33,65},{65,33},{34,66},{66,34},{35,67},{67,35},{3... | collective-permute-start | bytes 786440 | tf_op jit(solution)/shard_map/ppermute | solution.py:440
  39.7 0.7 copy-start.1
  47.6 2.0 %collective-permute-start.6 = (f32[16,24,256]{2,1,0:T(8,128)}, f32[16,24,256]{2,1,0:T(8,128)S(1)}, u32[]{:S(2)}, u32[]{:S(2)}) collective-permute-start(f32[16,24,256]{2,1,0:T(8,128)} %get-tuple-element.30), channel_id=1, source_target_pairs={{0,1},{1,0},{2,3},{3,2},{4,5},{5,4},{6,7},{7,6},{8,9},{9,8},{10,11... | collective-permute-start | bytes 1179656 | tf_op jit(solution)/shard_map/ppermute | solution.py:443
  73.2 3.8 %collective-permute-start.7 = (f32[24,256]{1,0:T(8,128)S(1)}, f32[24,256]{1,0:T(8,128)S(1)}, u32[]{:S(2)}, u32[]{:S(2)}) collective-permute-start(f32[24,256]{1,0:T(8,128)S(1)} %reduce_sum.9), channel_id=1, source_target_pairs={{0,32},{32,0},{64,96},{96,64},{1,33},{33,1},{65,97},{97,65},{2,34}... | collective-permute-start | bytes 73736 | tf_op jit(solution)/shard_map/ppermute | solution.py:443
  77.0 3.9 %collective-permute-start.8 = (f32[24,256]{1,0:T(8,128)S(1)}, f32[24,256]{1,0:T(8,128)S(1)}, u32[]{:S(2)}, u32[]{:S(2)}) collective-permute-start(f32[24,256]{1,0:T(8,128)S(1)} %add.25), channel_id=1, source_target_pairs={{0,96},{32,64},{64,32},{96,0},{1,97},{33,65},{65,33},{97,1},{2,98}... | collective-permute-start | bytes 73736 | tf_op jit(solution)/shard_map/ppermute | solution.py:443
  93.1 6.0 %collective-permute-start.9 = (f32[16,24,256]{2,1,0:T(8,128)S(1)}, f32[16,24,256]{2,1,0:T(8,128)S(1)}, u32[]{:S(2)}, u32[]{:S(2)}) collective-permute-start(f32[16,24,256]{2,1,0:T(8,128)S(1)} %all_to_all.11), channel_id=1, source_target_pairs={{0,1},{1,0},{2,3},{3,2},{4,5},{5,4},{6,7},{7,6},{8,9},{9,8},{10,11... | collective-permute-start | bytes 1179656 | tf_op jit(solution)/shard_map/ppermute | solution.py:443
